TPU v7x, 32 devices: a whole 2x2x4 slice. The times are simulated.
32 devices in a mesh: groups: 2 (over x), vocab: 8 (over z, y), tokens: 2 (over core).
Axes of the slice: x: 2, y: 2, z: 4, core: 2. Of those that a mesh axis runs over, the one named last changes fastest.
Arguments:
- teacher_hidden: bfloat16 [2048, 4608], P(('groups', 'vocab', 'tokens')), parts along dimension 0, may hold values from -24 to 24
- route: int32 [32], P('groups'), parts along dimension 0, may hold values from 0 to 15, each once
- teacher_head: bfloat16 [4608, 16000], P('tokens', 'vocab'), may hold values from -0.09375 to 0.09375
- student_logits: bfloat16 [2048, 16000], P(('groups', 'tokens'), 'vocab'), parts along dimension 0, may hold values from -40 to 40
- targets: int32 [2048], P(('groups', 'tokens')), parts along dimension 0, may hold values from 0 to 15999
Outputs:
- gradient: bfloat16 [2048, 16000], P(('groups', 'tokens'), 'vocab'), parts along dimension 0
- token_loss: float32 [2048], P(('groups', 'tokens')), parts along dimension 0
There are 2 independent parts, one for each index of `groups`. A program takes and returns all parts, laid end to end along the dimension named above; an argument that names none is the same for every part. Nothing has to cross between parts.
Inputs may be any that keep to these rules, and one draw needn't show every extreme that they name: route is a permutation of 0 to 15.
All inputs are finite; a program needn't handle non-finite values.
Results may differ from a plain program's by a relative error of at most 0.001.
Values may be sent and summed in bfloat16 or wider, within the bound.
A program may use at most 64 MiB of HBM per device.

v0:
```python
import jax
import jax.numpy as jnp
from jax import lax
from jax.sharding import PartitionSpec as P

BLOCK_ROWS = 64


SOFT_CAP = 30.0
MIX_WEIGHT = 0.5


def from_partner(value, axis, bit):
    mask = 2**bit
    pairs = [(source, source ^ mask) for source in range(lax.axis_size(axis))]
    return lax.ppermute(value, axis, pairs)


def capped_of(values):
    return SOFT_CAP * jnp.tanh(values / SOFT_CAP)


def logit_terms(features, weights):
    return jnp.dot(features, weights, preferred_element_type=jnp.float32)


def per_device(teacher_hidden, route, teacher_head, student_logits, targets):
    row_count, col_count = student_logits.shape
    head_rows = teacher_head.shape[0]
    token_index = lax.axis_index("tokens")
    vocab_index = lax.axis_index("vocab")
    capped = capped_of(student_logits.astype(jnp.float32))
    exp_student = jnp.exp(capped)
    columns = vocab_index * col_count + lax.broadcasted_iota(jnp.int32, (1, col_count), 1)
    target_hits = targets[:, None] == columns
    picked_part = jnp.sum(jnp.where(target_hits, capped, 0.0), axis=1)
    student_part = jnp.sum(exp_student, axis=1)
    own_half = lax.dynamic_slice_in_dim(teacher_hidden, token_index * head_rows, head_rows, 1)
    given_half = lax.dynamic_slice_in_dim(
        teacher_hidden, (1 - token_index) * head_rows, head_rows, 1
    )
    received = from_partner(given_half, "tokens", 0)
    lower_rows = jnp.where(token_index == 0, own_half, received)
    upper_rows = jnp.where(token_index == 0, received, own_half)
    paired = jnp.concatenate((lower_rows, upper_rows), axis=0)
    sliced = lax.all_gather(paired, "vocab", axis=0, tiled=True)
    half_blocks = sliced.reshape(-1, BLOCK_ROWS, head_rows)
    features = jnp.take(half_blocks, route, axis=0).reshape(-1, head_rows)
    teacher_raw = lax.psum_scatter(
        logit_terms(features, teacher_head), "tokens", scatter_dimension=0, tiled=True
    )
    teacher_capped = capped_of(teacher_raw)
    exp_teacher = jnp.exp(teacher_capped)
    teacher_part = jnp.sum(exp_teacher, axis=1)
    cross_part = jnp.sum(exp_teacher * (teacher_capped - capped), axis=1)
    student_total, picked, teacher_total, cross_sum = lax.psum(
        (student_part, picked_part, teacher_part, cross_part), "vocab"
    )
    log_student = jnp.log(student_total)
    token_loss = MIX_WEIGHT * (cross_sum / teacher_total - jnp.log(teacher_total) + log_student) + (
        1.0 - MIX_WEIGHT
    ) * (log_student - picked)
    cap_slope = 1.0 - (capped / SOFT_CAP) ** 2
    gradient = (
        exp_student / student_total[:, None]
        - MIX_WEIGHT * exp_teacher / teacher_total[:, None]
        - (1.0 - MIX_WEIGHT) * target_hits.astype(jnp.float32)
    ) * cap_slope
    return (gradient.astype(jnp.bfloat16), token_loss)


def solution(mesh):
    return jax.shard_map(
        per_device,
        mesh=mesh,
        in_specs=(
            P(("groups", "vocab", "tokens"), None),
            P("groups"),
            P("tokens", "vocab"),
            P(("groups", "tokens"), "vocab"),
            P(("groups", "tokens")),
        ),
        out_specs=(P(("groups", "tokens"), "vocab"), P(("groups", "tokens"))),
        check_vma=False,
    )
```

profile of v0, /device:TPU:0, one launch (start us, length us, event | category | flops | bytes accessed | tf_op | source)
XLA Modules:
  0.0 172.0 jit_solution(4229314055386310183)
XLA Ops:
  7.2 0.0 all-gather.2.cloned.1.call-start
  7.2 1.0 constant_dynamic-slice_fusion
  8.2 0.5 collective-permute-start
  8.7 1.2 collective-permute-done
  9.9 1.1 broadcast_select_fusion.1
  11.0 0.9 pad_maximum_fusion
  11.8 0.0 all-gather.2.cloned.1.call-update
  11.9 0.0 reduce-scatter.2.cloned.1.call-start
  11.9 0.7 compare_and_fusion
  12.6 0.1 broadcast_in_dim.21
  12.7 0.1 broadcast_in_dim.22
  12.8 0.7 compare_select_fusion.2
  13.4 81.1 %all-gather.2.cloned.1.call-done = bf16[1024,2304]{1,0:T(8,128)(2,1)} async-done(((bf16[128,2304]{1,0:T(8,128)(2,1)}), bf16[1024,2304]{1,0:T(8,128)(2,1)}) %all-gather.2.cloned.1.call-update) | async-done | bytes 4718608 | tf_op jit(solution)/shard_map/all_gather | solution.py:46
  94.5 5.4 %gather_fusion = bf16[16,64,2304]{2,1,0:T(8,128)(2,1)} fusion(bf16[16,64,2304]{2,1,0:T(8,128)(2,1)} %bitcast.5, s32[1024]{0:T(1024)S(1)} %pad_clamp_fusion), kind=kCustom, calls=%fused_computation | custom fusion | bytes 9437248 | tf_op jit(solution)/shard_map/jit(_take)/gather | solution.py:48
  99.9 2.8 %bitcast_select_fusion = bf16[1024,2304]{1,0:T(8,128)(2,1)S(1)} fusion(bf16[16,64,2304]{2,1,0:T(8,128)(2,1)} %gather_fusion, pred[1024]{0:T(1024)(128)(4,1)S(1)} %broadcast_in_dim.22), kind=kLoop, calls=%fused_computation.3 | loop fusion | flops 2359296 | bytes 9438208 | tf_op jit(solution)/shard_map/jit(_take)/select_n | solution.py:48
  102.7 14.2 %fusion.7 = f32[1024,2000]{0,1:T(8,128)} fusion(bf16[1024,2304]{1,0:T(8,128)(2,1)S(1)} %bitcast_select_fusion, bf16[2304,2000]{0,1:T(8,128)(2,1)} %param.7), kind=kOutput, calls=%fused_computation.24 | convolution fusion | flops 9437184000 | bytes 22126592 | tf_op jit(solution)/shard_map/dot_general | solution.py:24
  116.9 0.0 copy-start
  116.9 0.0 copy-start.1
  116.9 0.0 reduce-scatter.2.cloned.1.call-update
  116.9 14.9 %reduce-scatter.2.cloned.1.call-done = f32[512,2000]{0,1:T(8,128)} async-done(((f32[1024,2000]{0,1:T(8,128)}), f32[512,2000]{0,1:T(8,128)}) %reduce-scatter.2.cloned.1.call-update) | async-done | bytes 4096016 | tf_op jit(solution)/shard_map/reduce_scatter | solution.py:49
  131.9 0.0 copy-done
  131.9 0.0 copy-done.1
  131.9 4.8 %multiply_reduce_fusion = (f32[512]{0:T(512)S(1)}, f32[512]{0:T(512)S(1)}, f32[512]{0:T(512)S(1)}, f32[512]{0:T(512)S(1)}) fusion(bf16[512,2000]{0,1:T(8,128)(2,1)S(1)} %copy-done, f32[512,2000]{0,1:T(8,128)} %reduce-scatter.2.cloned.1.call-done, s32[2000]{0:T(1024)S(1)} %iota_add_fusion, s32[512]{0:T(512)S(1)} %copy-done.1), kind=kLoop, calls=%fused_computation.8 | loop fusion | flops 13309952 | bytes 6162240 | tf_op jit(solution)/shard_map/reduce_sum | solution.py:55
  136.6 21.9 %all-reduce = (f32[512]{0:T(512)S(1)}, f32[512]{0:T(512)S(1)}, f32[512]{0:T(512)S(1)}, f32[512]{0:T(512)S(1)}) all-reduce(f32[512]{0:T(512)S(1)} %get-tuple-element.3, f32[512]{0:T(512)S(1)} %get-tuple-element.5, f32[512]{0:T(512)S(1)} %get-tuple-element.4, ...), channel_id=1, replica_groups=mesh['groups'=2,'vocab'=8,'tokens'=2] {'vocab'}, use_global_device_ids=true, to_apply=%region_4.5 | all-reduce | flops 2048 | bytes 16384 | tf_op jit(solution)/shard_map/psum | solution.py:56
  158.6 0.6 add_multiply_fusion
  159.2 6.0 %fusion.2 = bf16[512,2000]{0,1:T(8,128)(2,1)} fusion(bf16[512,2000]{0,1:T(8,128)(2,1)S(1)} %copy-done, f32[512,2000]{0,1:T(8,128)} %reduce-scatter.2.cloned.1.call-done, s32[512]{0:T(512)S(1)} %copy-done.1, f32[512]{0:T(512)S(1)} %get-tuple-element.6, f32[512]{0:T(512)S(1)} %get-tuple-element.7, s32[2000]{0:T(1024)S(1)} %iota_add_fusion), kind=kLoop, calls=%fused_computation.6 | loop fusion | flops 16384000 | bytes 8206144 | tf_op jit(solution)/shard_map/convert_element_type | solution.py:69
  (2 shorter events, 0.0 us)
Async XLA Ops:
  7.2 87.4 %all-gather.2.cloned.1.call-start = ((), (), s32[]{:S(2)}) async-start(), calls=%async_computation.1 | async-start | bytes 5308416 | tf_op jit(solution)/shard_map/all_gather | solution.py:46
  8.2 1.7 %collective-permute-start = (bf16[64,2304]{1,0:T(8,128)(2,1)S(1)}, bf16[64,2304]{1,0:T(8,128)(2,1)S(1)}, u32[]{:S(2)}, u32[]{:S(2)}) collective-permute-start(bf16[64,2304]{1,0:T(8,128)(2,1)S(1)} %constant_dynamic-slice_fusion), channel_id=1, source_target_pairs={{0,1},{1,0},{2,3},{3,2},{4,5},{5,4},{6,7},{7,6},{8,9},{9,8},{10,11... | collective-permute-start | bytes 884744 | tf_op jit(solution)/shard_map/ppermute | solution.py:16
  11.9 120.0 %reduce-scatter.2.cloned.1.call-start = ((), (), s32[]{:S(2)}) async-start(), calls=%async_computation.2 | async-start | bytes 12288000 | tf_op jit(solution)/shard_map/reduce_scatter | solution.py:49
  116.9 15.0 %copy-start = (bf16[512,2000]{0,1:T(8,128)(2,1)S(1)}, bf16[512,2000]{0,1:T(8,128)(2,1)}, u32[]{:S(2)}) copy-start(bf16[512,2000]{0,1:T(8,128)(2,1)} %param.8) | copy-start | bytes 6144004
  116.9 15.0 %copy-start.1 = (s32[512]{0:T(512)S(1)}, s32[512]{0:T(512)}, u32[]{:S(2)}) copy-start(s32[512]{0:T(512)} %param.9) | copy-start | bytes 6148
Sparse Core Ops, SparseCore 0:
  12.0 82.4 all-gather.1
  117.0 14.7 reduce-scatter.1
where the time goes:
time: 172 us
  waiting for transfers between devices  97.3 us (57%)
  blocking collectives  21.9 us (13%)
  other arithmetic  17.4 us (10%)
  matrix products  14.2 us (8%)
  between operations  14.1 us (8%)
  local copies, waits for them, and re-layouts  6.51 us (4%)
    all_gather x1, waiting for transfers between devices, per_device(): sliced = lax.all_gather(paired, 'vocab', axis=0, tiled=True)  81.1 us
    psum x1, blocking collectives, per_device(): lax.psum((student_part, picked_part, teacher_part, cross_part), 'vocab')  21.9 us
    reduce_scatter x1, waiting for transfers between devices, per_device(): lax.psum_scatter(logit_terms(features, teacher_head), 'tokens', scatter_d...  14.9 us
    dot_general x1, matrix products, logit_terms(): return jnp.dot(features, weights, preferred_element_type=jnp.float32)  14.2 us
    convert_element_type x1, other arithmetic, per_device(): return (gradient.astype(jnp.bfloat16), token_loss)  6.01 us
    gather x1, local copies, waits for them, and re-layouts, per_device(): features = jnp.take(half_blocks, route, axis=0).reshape(-1, head_rows)  5.35 us
    reduce_sum x1, other arithmetic, per_device(): cross_part = jnp.sum(exp_teacher * (teacher_capped - capped), axis=1)  4.76 us
    select_n x2, other arithmetic, per_device(): features = jnp.take(half_blocks, route, axis=0).reshape(-1, head_rows)  3.48 us
  transfers between devices with their start and end apart: 3, of which 3 were waited for; matrix products, arithmetic and copies ran while one was open for 1% of the time, Pallas kernels for 0%

commit v1 on v0

--- a/solution.py
+++ b/solution.py
@@ -1,6 +1,8 @@
 import jax
 import jax.numpy as jnp
 from jax import lax
+from jax.experimental import pallas as pl
+from jax.experimental.pallas import tpu as pltpu
 from jax.sharding import PartitionSpec as P
 
 BLOCK_ROWS = 64
@@ -69,9 +71,373 @@
     return (gradient.astype(jnp.bfloat16), token_loss)
 
 
+MESH = pl.DeviceIdType.MESH
+ROWS = 16
+LINE = 4
+COLUMN_TILE = 512
+
+
+def fused_kernel(
+    hidden, route, head, student, targets,
+    gradient, loss,
+    head_v, feats, own_p, other_p, student_v, capped_v, exp_t, grad_v, target_v,
+    stat, stat_all, stat_cols,
+    load_sem, send_sem, recv_sem, part_send, part_recv, stat_send, stat_recv, store_sem,
+):
+    c = lax.axis_index("tokens")
+    v = lax.axis_index("vocab")
+    z = v // 2
+    y = v - 2 * z
+    unit = hidden.shape[0]
+    depth = head.shape[0]
+    cols = head.shape[1]
+    token_rows = student.shape[0]
+    peers = 2 * LINE
+    partner = {"vocab": v, "tokens": 1 - c}
+
+    def slot_of(zs, ys, s):
+        return (zs * 2 + ys) * 2 + (c + s - 2 * c * s)
+
+    def rows_of(slot):
+        return pl.ds(pl.multiple_of(slot * unit, unit), unit)
+
+    def half(which):
+        return pl.ds(pl.multiple_of(which * depth, 128), depth)
+
+    own_slot = slot_of(z, y, 0)
+    load_own = pltpu.make_async_copy(hidden.at[:, half(c)], feats.at[rows_of(own_slot)], load_sem.at[0])
+    load_head = pltpu.make_async_copy(head, head_v, load_sem.at[1])
+    load_student = pltpu.make_async_copy(student, student_v, load_sem.at[2])
+    load_target = pltpu.make_async_copy(targets, target_v, load_sem.at[3])
+    load_own.start()
+
+    barrier = pltpu.get_barrier_semaphore()
+    pl.semaphore_signal(barrier, inc=1, device_id=partner, device_id_type=MESH)
+    for d in range(1, peers):
+        peer = {"vocab": lax.rem(v + d, peers), "tokens": c}
+        pl.semaphore_signal(barrier, inc=1, device_id=peer, device_id_type=MESH)
+    pl.semaphore_wait(barrier, peers)
+
+    def partner_copy():
+        return pltpu.make_async_remote_copy(
+            src_ref=hidden.at[:, half(1 - c)],
+            dst_ref=feats.at[rows_of(own_slot)],
+            send_sem=send_sem.at[3, own_slot],
+            recv_sem=recv_sem.at[own_slot],
+            device_id=partner,
+            device_id_type=MESH,
+        )
+
+    def unit_copy(way, slot):
+        target = (v + 2, v - 2, v + 1 - 2 * y)[way]
+        return pltpu.make_async_remote_copy(
+            src_ref=feats.at[rows_of(slot)],
+            dst_ref=feats.at[rows_of(slot)],
+            send_sem=send_sem.at[way, slot],
+            recv_sem=recv_sem.at[slot],
+            device_id={"vocab": target, "tokens": c},
+            device_id_type=MESH,
+        )
+
+    def arrived(slot):
+        unit_copy(2, slot).wait_recv()
+
+    def send_line(way, slot):
+        @pl.when(z < LINE - 1 if way == 0 else z > 0)
+        def _():
+            unit_copy(way, slot).start()
+
+    def part_copy(block):
+        rows = pl.ds(2 * block, 2)
+        return pltpu.make_async_remote_copy(
+            src_ref=own_p.at[rows],
+            dst_ref=other_p.at[rows],
+            send_sem=part_send.at[block],
+            recv_sem=part_recv.at[block],
+            device_id=partner,
+            device_id_type=MESH,
+        )
+
+    def multiply(block):
+        rows = pl.ds(pl.multiple_of(block * 2 * unit, 2 * unit), 2 * unit)
+        for first in range(0, cols, COLUMN_TILE):
+            width = min(COLUMN_TILE, cols - first)
+            own_p[pl.ds(2 * block, 2), :, first : first + width] = jnp.dot(
+                feats[rows, :], head_v[:, first : first + width], preferred_element_type=jnp.float32
+            ).reshape(2, unit, width)
+        part_copy(block).start()
+
+    partner_copy().start()
+    load_own.wait()
+    send_line(0, own_slot)
+    send_line(1, own_slot)
+    unit_copy(2, own_slot).start()
+    load_head.start()
+    load_student.start()
+    load_target.start()
+    own_second = slot_of(z, y, 1)
+    arrived(own_second)
+    send_line(0, own_second)
+    send_line(1, own_second)
+    unit_copy(2, own_second).start()
+
+    load_student.wait()
+    load_target.wait()
+    columns = v * cols + lax.broadcasted_iota(jnp.int32, (1, cols), 1)
+    lane = lax.broadcasted_iota(jnp.int32, (ROWS, 128), 1)
+
+    def student_pass(i, carry):
+        rows = pl.ds(pl.multiple_of(i * ROWS, ROWS), ROWS)
+        capped = capped_of(student_v[rows, :].astype(jnp.float32))
+        capped_v[rows, :] = capped
+        total = jnp.sum(jnp.exp(capped), axis=1, keepdims=True)
+        picked = jnp.sum(jnp.where(target_v[rows, :] == columns, capped, 0.0), axis=1, keepdims=True)
+        stat_cols[rows, :] = jnp.where(lane == 0, total, jnp.where(lane == 1, picked, 0.0))
+        return carry
+
+    passes = token_rows // ROWS
+    load_head.wait()
+    multiply(v)
+
+    def step(k, carry):
+        for s in range(2):
+            src = z - 1 - k
+
+            @pl.when(src >= 0)
+            def _():
+                slot = slot_of(src, y, s)
+                arrived(slot)
+                send_line(0, slot)
+
+                @pl.when((src > 0) if s else (src >= 0))
+                def _():
+                    unit_copy(2, slot).start()
+
+            src_up = z + 1 + k
+
+            @pl.when(src_up <= LINE - 1)
+            def _():
+                slot = slot_of(src_up, y, s)
+                arrived(slot)
+                send_line(1, slot)
+
+                @pl.when((src_up < LINE - 1) if s else (src_up <= LINE - 1))
+                def _():
+                    unit_copy(2, slot).start()
+
+            if s == 0:
+                @pl.when((z == k) & (z > 0))
+                def _():
+                    slot = slot_of(0, 1 - y, 1)
+                    arrived(slot)
+                    send_line(0, slot)
+
+                @pl.when((LINE - 1 - z == k) & (z < LINE - 1))
+                def _():
+                    slot = slot_of(LINE - 1, 1 - y, 1)
+                    arrived(slot)
+                    send_line(1, slot)
+
+            across = z - k
+
+            @pl.when((across >= 0) & ((s == 0) | (across > 0) | (k == 0)))
+            def _():
+                slot = slot_of(across, 1 - y, s)
+                arrived(slot)
+                if s == 1:
+                    @pl.when((k == 0) & (z == 0))
+                    def _():
+                        unit_copy(0, slot).start()
+
+                    @pl.when((k == 0) & (z == LINE - 1))
+                    def _():
+                        unit_copy(1, slot).start()
+
+            across_up = z + k
+
+            @pl.when((k > 0) & (across_up <= LINE - 1) & ((s == 0) | (across_up < LINE - 1)))
+            def _():
+                arrived(slot_of(across_up, 1 - y, s))
+
+        def products(which, inner):
+            zs = jnp.where(which == 0, z - 1 - k, jnp.where(which == 1, z + 1 + k, jnp.where(which == 2, z - k, z + k)))
+            ys = jnp.where(which < 2, y, 1 - y)
+
+            @pl.when((zs >= 0) & (zs <= LINE - 1) & ((which < 3) | (k > 0)))
+            def _():
+                multiply(zs * 2 + ys)
+
+            return inner
+
+        lax.fori_loop(0, 4, products, 0)
+
+        @pl.when(k < LINE - 1)
+        def _():
+            lax.fori_loop(k * passes // (LINE - 1), (k + 1) * passes // (LINE - 1), student_pass, 0)
+
+        return carry
+
+    lax.fori_loop(0, LINE, step, 0)
+
+    def await_part(block, carry):
+        part_copy(block).wait_recv()
+        return carry
+
+    lax.fori_loop(0, peers, await_part, 0)
+
+    per_block = BLOCK_ROWS // ROWS
+    first_block = c * (token_rows // BLOCK_ROWS)
+
+    def teacher_pass(i, carry):
+        block = i // per_block
+        inside = i - block * per_block
+        rows = pl.ds(pl.multiple_of(i * ROWS, ROWS), ROWS)
+        source = route[first_block + block]
+        within = pl.ds(pl.multiple_of(inside * ROWS, ROWS), ROWS)
+        teacher = capped_of(own_p[source, within, :] + other_p[source, within, :])
+        grown = jnp.exp(teacher)
+        exp_t[rows, :] = grown
+        total = jnp.sum(grown, axis=1, keepdims=True)
+        cross = jnp.sum(grown * (teacher - capped_v[rows, :]), axis=1, keepdims=True)
+        before = stat_cols[rows, :]
+        stat_cols[rows, :] = jnp.where(lane == 2, total, jnp.where(lane == 3, cross, before))
+        return carry
+
+    lax.fori_loop(0, passes, teacher_pass, 0)
+    stat[...] = jnp.transpose(stat_cols[...])[0:8, :]
+
+    def stat_copy(peer, slot):
+        return pltpu.make_async_remote_copy(
+            src_ref=stat,
+            dst_ref=stat_all.at[slot],
+            send_sem=stat_send.at[peer],
+            recv_sem=stat_recv.at[slot],
+            device_id={"vocab": peer, "tokens": c},
+            device_id_type=MESH,
+        )
+
+    for d in range(1, peers):
+        stat_copy(lax.rem(v + d, peers), v).start()
+    stat_all[v] = stat[...]
+    for d in range(1, peers):
+        stat_copy(0, lax.rem(v + d, peers)).wait_recv()
+    sums = stat_all[0]
+    for d in range(1, peers):
+        sums = sums + stat_all[d]
+    log_student = jnp.log(sums[0:1, :])
+    loss[...] = MIX_WEIGHT * (sums[3:4, :] / sums[2:3, :] - jnp.log(sums[2:3, :]) + log_student) + (
+        1.0 - MIX_WEIGHT
+    ) * (log_student - sums[1:2, :])
+    scales = jnp.concatenate([1.0 / sums[0:1, :], MIX_WEIGHT / sums[2:3, :]], axis=0)
+    scales = jnp.concatenate([scales, jnp.zeros((126, token_rows), jnp.float32)], axis=0)
+    stat_cols[...] = jnp.transpose(scales)
+
+    def gradient_pass(i, carry):
+        rows = pl.ds(pl.multiple_of(i * ROWS, ROWS), ROWS)
+        capped = capped_v[rows, :]
+        hits = jnp.where(target_v[rows, :] == columns, 1.0 - MIX_WEIGHT, 0.0)
+        scale = stat_cols[rows, :]
+        value = jnp.exp(capped) * scale[:, 0:1] - exp_t[rows, :] * scale[:, 1:2] - hits
+        slope = 1.0 - (capped / SOFT_CAP) ** 2
+        grad_v[rows, :] = (value * slope).astype(grad_v.dtype)
+        return carry
+
+    pieces = 4
+    piece_rows = token_rows // pieces
+    for p in range(pieces):
+        lax.fori_loop(p * passes // pieces, (p + 1) * passes // pieces, gradient_pass, 0)
+        rows = pl.ds(p * piece_rows, piece_rows)
+        pltpu.make_async_copy(grad_v.at[rows], gradient.at[rows], store_sem.at[p]).start()
+
+    partner_copy().wait_send()
+    for s in range(2):
+        def sent(zs, carry):
+            slot = slot_of(zs, y, s)
+
+            @pl.when((z < LINE - 1) & (zs <= z))
+            def _():
+                unit_copy(0, slot).wait_send()
+
+            @pl.when((z > 0) & (zs >= z))
+            def _():
+                unit_copy(1, slot).wait_send()
+
+            @pl.when((zs == z) | (s == 0) | ((zs > 0) & (zs < LINE - 1)))
+            def _():
+                unit_copy(2, slot).wait_send()
+
+            return carry
+
+        lax.fori_loop(0, LINE, sent, 0)
+
+    @pl.when(z < LINE - 1)
+    def _():
+        unit_copy(0, slot_of(0, 1 - y, 1)).wait_send()
+
+    @pl.when(z > 0)
+    def _():
+        unit_copy(1, slot_of(LINE - 1, 1 - y, 1)).wait_send()
+
+    def sent_part(block, carry):
+        part_copy(block).wait_send()
+        return carry
+
+    lax.fori_loop(0, peers, sent_part, 0)
+    for d in range(1, peers):
+        stat_copy(lax.rem(v + d, peers), v).wait_send()
+    for p in range(pieces):
+        rows = pl.ds(p * piece_rows, piece_rows)
+        pltpu.make_async_copy(grad_v.at[rows], gradient.at[rows], store_sem.at[p]).wait()
+
+
+def fused(teacher_hidden, route, teacher_head, student_logits, targets):
+    tokens, cols = student_logits.shape
+    depth = teacher_head.shape[0]
+    unit = teacher_hidden.shape[0]
+    units = 4 * LINE
+    anywhere = pl.BlockSpec(memory_space=pl.ANY)
+    dma = pltpu.SemaphoreType.DMA
+    gradient, loss = pl.pallas_call(
+        fused_kernel,
+        out_shape=(
+            jax.ShapeDtypeStruct((tokens, cols), jnp.bfloat16),
+            jax.ShapeDtypeStruct((1, tokens), jnp.float32),
+        ),
+        in_specs=[anywhere, pl.BlockSpec(memory_space=pltpu.SMEM), anywhere, anywhere, anywhere],
+        out_specs=(anywhere, pl.BlockSpec(memory_space=pltpu.VMEM)),
+        scratch_shapes=[
+            pltpu.VMEM((depth, cols), jnp.bfloat16),
+            pltpu.VMEM((units * unit, depth), jnp.bfloat16),
+            pltpu.VMEM((units, unit, cols), jnp.float32),
+            pltpu.VMEM((units, unit, cols), jnp.float32),
+            pltpu.VMEM((tokens, cols), jnp.bfloat16),
+            pltpu.VMEM((tokens, cols), jnp.float32),
+            pltpu.VMEM((tokens, cols), jnp.float32),
+            pltpu.VMEM((tokens, cols), jnp.bfloat16),
+            pltpu.VMEM((tokens, 1), jnp.int32),
+            pltpu.VMEM((8, tokens), jnp.float32),
+            pltpu.VMEM((2 * LINE, 8, tokens), jnp.float32),
+            pltpu.VMEM((tokens, 128), jnp.float32),
+            dma((4,)),
+            dma((4, units)),
+            dma((units,)),
+            dma((2 * LINE,)),
+            dma((2 * LINE,)),
+            dma((2 * LINE,)),
+            dma((2 * LINE,)),
+            dma((4,)),
+        ],
+        compiler_params=pltpu.CompilerParams(
+            collective_id=0, has_side_effects=True, vmem_limit_bytes=56 * 2**20
+        ),
+    )(teacher_hidden, route, teacher_head, student_logits, targets[:, None])
+    return gradient, loss.reshape(tokens)
+
+
 def solution(mesh):
+    body = fused if mesh.shape["vocab"] == 2 * LINE else per_device
     return jax.shard_map(
-        per_device,
+        body,
         mesh=mesh,
         in_specs=(
             P(("groups", "vocab", "tokens"), None),

time: 172 us -> 93.3 us (0.54); the launches traced: 172 us -> 91.5 us
  waiting for transfers between devices: 97.3 us -> 0 us
  Pallas kernels: 0 us -> 68.2 us
  blocking collectives: 21.9 us -> 0 us
  other arithmetic: 17.4 us -> 0 us
  local copies, waits for them, and re-layouts: 6.51 us -> 22.7 us
  matrix products: 14.2 us -> 0 us
  between operations: 14.1 us -> 0.65 us
    all_gather x1 -> x0, waiting for transfers between devices: 81.1 us -> none  [per_device(): sliced = lax.all_gather(paired, 'vocab', axis=0, tiled=True)]
    pallas_call x0 -> x1, Pallas kernels: none -> 68.2 us  [fused(): pl.pallas_call(fused_kernel, out_shape=(jax.ShapeDtypeStruct((tokens, col...]
    psum x1 -> x0, blocking collectives: 21.9 us -> none  [per_device(): lax.psum((student_part, picked_part, teacher_part, cross_part), 'vocab')]
    unnamed x4 -> x6, local copies, waits for them, and re-layouts: 0.01 us -> 21.1 us
    reduce_scatter x1 -> x0, waiting for transfers between devices: 14.9 us -> none  [per_device(): lax.psum_scatter(logit_terms(features, teacher_head), 'tokens', scatter_d...]
    dot_general x1 -> x0, matrix products: 14.2 us -> none  [logit_terms(): return jnp.dot(features, weights, preferred_element_type=jnp.float32)]
    convert_element_type x1 -> x0, other arithmetic: 6.01 us -> none  [per_device(): return (gradient.astype(jnp.bfloat16), token_loss)]
    gather x1 -> x0, local copies, waits for them, and re-layouts: 5.35 us -> none  [per_device(): features = jnp.take(half_blocks, route, axis=0).reshape(-1, head_rows)]
  transfers between devices with their start and end apart: 3 -> 0, of which waited for: 3 -> 0; matrix products, arithmetic and copies ran while one was open for 1% -> 0% of each run, Pallas kernels for 0% -> 0%
where the time goes in v1:
time: 93.3 us; the launch traced here: 91.5 us
  Pallas kernels  68.2 us (73%)
  local copies, waits for them, and re-layouts  22.7 us (24%)
    pallas_call x1, Pallas kernels, fused(): pl.pallas_call(fused_kernel, out_shape=(jax.ShapeDtypeStruct((tokens, col...  68.2 us
    unnamed x6, local copies, waits for them, and re-layouts  21.1 us

profile of v1, /device:TPU:0, one launch (start us, length us, event | category | flops | bytes accessed | tf_op | source)
XLA Modules:
  0.0 91.5 jit_solution(16686957131573050675)
XLA Ops:
  0.6 1.5 %copy.12.targets = s32[512,1]{1,0:T(8,128)} copy(s32[512,1]{0,1:T(1,128)} %bitcast.2) | data formatting | bytes 4096 | tf_op jit(solution)/shard_map/broadcast_in_dim | solution.py:433
  2.2 3.9 %copy.11.student = bf16[512,2000]{1,0:T(8,128)(2,1)} copy(bf16[512,2000]{0,1:T(8,128)(2,1)} %param.8) | data formatting | bytes 4096000 | tf_op args[3]
  6.1 12.7 %copy.10.head = bf16[2304,2000]{1,0:T(8,128)(2,1)} copy(bf16[2304,2000]{0,1:T(8,128)(2,1)} %param.7) | data formatting | bytes 18432000 | tf_op args[2]
  18.8 68.2 %shard_map.68 = (bf16[512,2000]{1,0:T(8,128)(2,1)}, f32[1,512]{1,0:T(1,128)}) custom-call(bf16[64,4608]{1,0:T(8,128)(2,1)} %hidden.1, s32[16]{0:T(128)} %route.1, bf16[2304,2000]{1,0:T(8,128)(2,1)} %copy.10.head, bf16[512,2000]{1,0:T(8,128)(2,1)} %copy.11.student, s32[512,1]{1,0:T(8,128)} %copy.12.targets), custom_call_target="tpu_custom_call" | custom-call | tf_op jit(solution)/shard_map/pallas_call | solution.py:400
  87.0 0.0 copy-start
  87.0 3.9 %copy.13 = bf16[512,2000]{0,1:T(8,128)(2,1)} copy(bf16[512,2000]{1,0:T(8,128)(2,1)} %get-tuple-element.8) | data formatting | bytes 4096000
  91.0 0.0 copy-done
  91.0 0.6 copy.15
Async XLA Ops:
  87.0 3.9 %copy-start = (f32[1,512]{1,0:T(1,128)S(1)}, f32[1,512]{1,0:T(1,128)}, u32[]{:S(2)}) copy-start(f32[1,512]{1,0:T(1,128)} %get-tuple-element.5) | copy-start | bytes 6148

commit v2 on v1

--- a/solution.py
+++ b/solution.py
@@ -72,16 +72,16 @@
 
 
 MESH = pl.DeviceIdType.MESH
-ROWS = 16
+ROWS = 80
 LINE = 4
-COLUMN_TILE = 512
+COLUMN_TILE = 400
 
 
 def fused_kernel(
     hidden, route, head, student, targets,
     gradient, loss,
-    head_v, feats, own_p, other_p, student_v, capped_v, exp_t, grad_v, target_v,
-    stat, stat_all, stat_cols,
+    head_v, feats, own_p, other_p, student_v, capped_v, exp_s, exp_t, grad_v, target_v,
+    stat, stat_all, sums_v,
     load_sem, send_sem, recv_sem, part_send, part_recv, stat_send, stat_recv, store_sem,
 ):
     c = lax.axis_index("tokens")
@@ -89,9 +89,8 @@
     z = v // 2
     y = v - 2 * z
     unit = hidden.shape[0]
-    depth = head.shape[0]
-    cols = head.shape[1]
-    token_rows = student.shape[0]
+    cols, depth = head.shape
+    token_rows = student.shape[1]
     peers = 2 * LINE
     partner = {"vocab": v, "tokens": 1 - c}
 
@@ -148,10 +147,9 @@
             unit_copy(way, slot).start()
 
     def part_copy(block):
-        rows = pl.ds(2 * block, 2)
         return pltpu.make_async_remote_copy(
-            src_ref=own_p.at[rows],
-            dst_ref=other_p.at[rows],
+            src_ref=own_p.at[block],
+            dst_ref=other_p.at[block],
             send_sem=part_send.at[block],
             recv_sem=part_recv.at[block],
             device_id=partner,
@@ -162,9 +160,12 @@
         rows = pl.ds(pl.multiple_of(block * 2 * unit, 2 * unit), 2 * unit)
         for first in range(0, cols, COLUMN_TILE):
             width = min(COLUMN_TILE, cols - first)
-            own_p[pl.ds(2 * block, 2), :, first : first + width] = jnp.dot(
-                feats[rows, :], head_v[:, first : first + width], preferred_element_type=jnp.float32
-            ).reshape(2, unit, width)
+            own_p[block, first : first + width, :] = lax.dot_general(
+                head_v[first : first + width, :],
+                feats[rows, :],
+                (((1,), (1,)), ((), ())),
+                preferred_element_type=jnp.float32,
+            )
         part_copy(block).start()
 
     partner_copy().start()
@@ -183,19 +184,24 @@
 
     load_student.wait()
     load_target.wait()
-    columns = v * cols + lax.broadcasted_iota(jnp.int32, (1, cols), 1)
-    lane = lax.broadcasted_iota(jnp.int32, (ROWS, 128), 1)
+    entry = lax.broadcasted_iota(jnp.int32, (ROWS, 1), 0) + v * cols
+
+    def rows8(values):
+        return jnp.sum(values.reshape(-1, 8, values.shape[-1]), axis=0)
+
+    sums_v[...] = jnp.zeros_like(sums_v)
 
     def student_pass(i, carry):
         rows = pl.ds(pl.multiple_of(i * ROWS, ROWS), ROWS)
         capped = capped_of(student_v[rows, :].astype(jnp.float32))
+        grown = jnp.exp(capped)
         capped_v[rows, :] = capped
-        total = jnp.sum(jnp.exp(capped), axis=1, keepdims=True)
-        picked = jnp.sum(jnp.where(target_v[rows, :] == columns, capped, 0.0), axis=1, keepdims=True)
-        stat_cols[rows, :] = jnp.where(lane == 0, total, jnp.where(lane == 1, picked, 0.0))
+        exp_s[rows, :] = grown
+        sums_v[0] += rows8(grown)
+        sums_v[1] += rows8(jnp.where(target_v[...] == entry + i * ROWS, capped, 0.0))
         return carry
 
-    passes = token_rows // ROWS
+    passes = cols // ROWS
     load_head.wait()
     multiply(v)
 
@@ -285,26 +291,36 @@
 
     lax.fori_loop(0, peers, await_part, 0)
 
-    per_block = BLOCK_ROWS // ROWS
-    first_block = c * (token_rows // BLOCK_ROWS)
-
-    def teacher_pass(i, carry):
-        block = i // per_block
-        inside = i - block * per_block
-        rows = pl.ds(pl.multiple_of(i * ROWS, ROWS), ROWS)
-        source = route[first_block + block]
-        within = pl.ds(pl.multiple_of(inside * ROWS, ROWS), ROWS)
-        teacher = capped_of(own_p[source, within, :] + other_p[source, within, :])
-        grown = jnp.exp(teacher)
-        exp_t[rows, :] = grown
-        total = jnp.sum(grown, axis=1, keepdims=True)
-        cross = jnp.sum(grown * (teacher - capped_v[rows, :]), axis=1, keepdims=True)
-        before = stat_cols[rows, :]
-        stat_cols[rows, :] = jnp.where(lane == 2, total, jnp.where(lane == 3, cross, before))
-        return carry
-
-    lax.fori_loop(0, passes, teacher_pass, 0)
-    stat[...] = jnp.transpose(stat_cols[...])[0:8, :]
+    first_block = c * (token_rows // unit)
+    lane = lax.broadcasted_iota(jnp.int32, (1, 2 * unit), 1)
+    low = lane < unit
+    tall = cols // 10
+    for pair in range(token_rows // (2 * unit)):
+        lanes = slice(pair * 2 * unit, (pair + 1) * 2 * unit)
+        left = route[first_block + 2 * pair]
+        right = route[first_block + 2 * pair + 1]
+        left_at, right_at = left // 2, right // 2
+        def teacher_pass(i, carry):
+            total, cross = carry
+            rows = pl.ds(pl.multiple_of(i * tall, 8), tall)
+            one = own_p[left_at, rows, :] + other_p[left_at, rows, :]
+            two = own_p[right_at, rows, :] + other_p[right_at, rows, :]
+            placed = jnp.where(low, one, two)
+            moved = pltpu.roll(jnp.where(low, two, one), unit, 1)
+            teacher = capped_of(jnp.where(stay, placed, moved))
+            grown = jnp.exp(teacher)
+            exp_t[rows, lanes] = grown
+            return total + rows8(grown), cross + rows8(grown * (teacher - capped_v[rows, lanes]))
+
+        stay = jnp.where(low, left - 2 * left_at, 1 - (right - 2 * right_at)) == 0
+        nothing = jnp.zeros((8, 2 * unit), jnp.float32)
+        total, cross = lax.fori_loop(0, 10, teacher_pass, (nothing, nothing))
+        sums_v[2, :, lanes] = total
+        sums_v[3, :, lanes] = cross
+
+    stat[...] = jnp.zeros_like(stat)
+    for which in range(4):
+        stat[which : which + 1, :] = jnp.sum(sums_v[which], axis=0, keepdims=True)
 
     def stat_copy(peer, slot):
         return pltpu.make_async_remote_copy(
@@ -328,22 +344,19 @@
     loss[...] = MIX_WEIGHT * (sums[3:4, :] / sums[2:3, :] - jnp.log(sums[2:3, :]) + log_student) + (
         1.0 - MIX_WEIGHT
     ) * (log_student - sums[1:2, :])
-    scales = jnp.concatenate([1.0 / sums[0:1, :], MIX_WEIGHT / sums[2:3, :]], axis=0)
-    scales = jnp.concatenate([scales, jnp.zeros((126, token_rows), jnp.float32)], axis=0)
-    stat_cols[...] = jnp.transpose(scales)
+    student_scale = 1.0 / sums[0:1, :]
+    teacher_scale = MIX_WEIGHT / sums[2:3, :]
 
     def gradient_pass(i, carry):
         rows = pl.ds(pl.multiple_of(i * ROWS, ROWS), ROWS)
-        capped = capped_v[rows, :]
-        hits = jnp.where(target_v[rows, :] == columns, 1.0 - MIX_WEIGHT, 0.0)
-        scale = stat_cols[rows, :]
-        value = jnp.exp(capped) * scale[:, 0:1] - exp_t[rows, :] * scale[:, 1:2] - hits
-        slope = 1.0 - (capped / SOFT_CAP) ** 2
+        hits = jnp.where(target_v[...] == entry + i * ROWS, 1.0 - MIX_WEIGHT, 0.0)
+        value = exp_s[rows, :] * student_scale - exp_t[rows, :] * teacher_scale - hits
+        slope = 1.0 - (capped_v[rows, :] / SOFT_CAP) ** 2
         grad_v[rows, :] = (value * slope).astype(grad_v.dtype)
         return carry
 
-    pieces = 4
-    piece_rows = token_rows // pieces
+    pieces = 5
+    piece_rows = cols // pieces
     for p in range(pieces):
         lax.fori_loop(p * passes // pieces, (p + 1) * passes // pieces, gradient_pass, 0)
         rows = pl.ds(p * piece_rows, piece_rows)
@@ -400,24 +413,25 @@
     gradient, loss = pl.pallas_call(
         fused_kernel,
         out_shape=(
-            jax.ShapeDtypeStruct((tokens, cols), jnp.bfloat16),
+            jax.ShapeDtypeStruct((cols, tokens), jnp.bfloat16),
             jax.ShapeDtypeStruct((1, tokens), jnp.float32),
         ),
         in_specs=[anywhere, pl.BlockSpec(memory_space=pltpu.SMEM), anywhere, anywhere, anywhere],
         out_specs=(anywhere, pl.BlockSpec(memory_space=pltpu.VMEM)),
         scratch_shapes=[
-            pltpu.VMEM((depth, cols), jnp.bfloat16),
+            pltpu.VMEM((cols, depth), jnp.bfloat16),
             pltpu.VMEM((units * unit, depth), jnp.bfloat16),
-            pltpu.VMEM((units, unit, cols), jnp.float32),
-            pltpu.VMEM((units, unit, cols), jnp.float32),
-            pltpu.VMEM((tokens, cols), jnp.bfloat16),
-            pltpu.VMEM((tokens, cols), jnp.float32),
-            pltpu.VMEM((tokens, cols), jnp.float32),
-            pltpu.VMEM((tokens, cols), jnp.bfloat16),
-            pltpu.VMEM((tokens, 1), jnp.int32),
+            pltpu.VMEM((units // 2, cols, 2 * unit), jnp.float32),
+            pltpu.VMEM((units // 2, cols, 2 * unit), jnp.float32),
+            pltpu.VMEM((cols, tokens), jnp.bfloat16),
+            pltpu.VMEM((cols, tokens), jnp.float32),
+            pltpu.VMEM((cols, tokens), jnp.float32),
+            pltpu.VMEM((cols, tokens), jnp.float32),
+            pltpu.VMEM((cols, tokens), jnp.bfloat16),
+            pltpu.VMEM((1, tokens), jnp.int32),
             pltpu.VMEM((8, tokens), jnp.float32),
             pltpu.VMEM((2 * LINE, 8, tokens), jnp.float32),
-            pltpu.VMEM((tokens, 128), jnp.float32),
+            pltpu.VMEM((4, 8, tokens), jnp.float32),
             dma((4,)),
             dma((4, units)),
             dma((units,)),
@@ -425,13 +439,13 @@
             dma((2 * LINE,)),
             dma((2 * LINE,)),
             dma((2 * LINE,)),
-            dma((4,)),
+            dma((5,)),
         ],
         compiler_params=pltpu.CompilerParams(
             collective_id=0, has_side_effects=True, vmem_limit_bytes=56 * 2**20
         ),
-    )(teacher_hidden, route, teacher_head, student_logits, targets[:, None])
-    return gradient, loss.reshape(tokens)
+    )(teacher_hidden, route, teacher_head.T, student_logits.T, targets[None, :])
+    return gradient.T, loss.reshape(tokens)
 
 
 def solution(mesh):

time: 93.3 us -> 75.6 us (0.81)
  local copies, waits for them, and re-layouts: 22.7 us -> 3.59 us
  Pallas kernels: 68.2 us -> 70 us
    unnamed x6 -> x4, local copies, waits for them, and re-layouts: 21.1 us -> 3.59 us
    pallas_call x1, Pallas kernels: 68.2 us -> 70 us  [fused(): pl.pallas_call(fused_kernel, out_shape=(jax.ShapeDtypeStruct((cols, token...]
    broadcast_in_dim x1 -> x0, local copies, waits for them, and re-layouts: 1.53 us -> none  [fused(): targets[:, None]]
where the time goes in v2:
time: 75.6 us; the launch traced here: 74.3 us
  Pallas kernels  70 us (93%)
  local copies, waits for them, and re-layouts  3.59 us (5%)
    pallas_call x1, Pallas kernels, fused(): pl.pallas_call(fused_kernel, out_shape=(jax.ShapeDtypeStruct((cols, token...  70 us
    unnamed x4, local copies, waits for them, and re-layouts  3.59 us

profile of v2, /device:TPU:0, one launch (start us, length us, event | category | flops | bytes accessed | tf_op | source)
XLA Modules:
  0.0 74.3 jit_solution(16735372562249253491)
XLA Ops:
  0.6 70.0 %shard_map.68 = (bf16[2000,512]{1,0:T(8,128)(2,1)}, f32[1,512]{1,0:T(1,128)}) custom-call(bf16[64,4608]{1,0:T(8,128)(2,1)} %hidden.1, s32[16]{0:T(128)} %route.1, bf16[2000,2304]{1,0:T(8,128)(2,1)} %bitcast.5, bf16[2000,512]{1,0:T(8,128)(2,1)} %bitcast.7, s32[1,512]{1,0:T(1,128)} %bitcast.8), custom_call_target="tpu_custom_call" | custom-call | tf_op jit(solution)/shard_map/pallas_call | solution.py:413
  70.7 0.0 copy-start
  70.7 3.0 %copy.9 = bf16[512,2000]{0,1:T(8,128)(2,1)} copy(bf16[512,2000]{0,1:T(8,128)(2,1)} %bitcast.6) | data formatting | bytes 4096000
  73.7 0.0 copy-done
  73.7 0.6 copy.10
Async XLA Ops:
  70.7 3.0 %copy-start = (f32[1,512]{1,0:T(1,128)S(1)}, f32[1,512]{1,0:T(1,128)}, u32[]{:S(2)}) copy-start(f32[1,512]{1,0:T(1,128)} %get-tuple-element.5) | copy-start | bytes 6148

commit v3 on v2

--- a/solution.py
+++ b/solution.py
@@ -109,6 +109,9 @@
     load_student = pltpu.make_async_copy(student, student_v, load_sem.at[2])
     load_target = pltpu.make_async_copy(targets, target_v, load_sem.at[3])
     load_own.start()
+    load_head.start()
+    load_student.start()
+    load_target.start()
 
     barrier = pltpu.get_barrier_semaphore()
     pl.semaphore_signal(barrier, inc=1, device_id=partner, device_id_type=MESH)
@@ -173,9 +176,6 @@
     send_line(0, own_slot)
     send_line(1, own_slot)
     unit_copy(2, own_slot).start()
-    load_head.start()
-    load_student.start()
-    load_target.start()
     own_second = slot_of(z, y, 1)
     arrived(own_second)
     send_line(0, own_second)
@@ -265,6 +265,11 @@
             def _():
                 arrived(slot_of(across_up, 1 - y, s))
 
+            if s == 0:
+                @pl.when(k < LINE - 1)
+                def _():
+                    lax.fori_loop(k * passes // (LINE - 1), (k + 1) * passes // (LINE - 1), student_pass, 0)
+
         def products(which, inner):
             zs = jnp.where(which == 0, z - 1 - k, jnp.where(which == 1, z + 1 + k, jnp.where(which == 2, z - k, z + k)))
             ys = jnp.where(which < 2, y, 1 - y)
@@ -276,10 +281,6 @@
             return inner
 
         lax.fori_loop(0, 4, products, 0)
-
-        @pl.when(k < LINE - 1)
-        def _():
-            lax.fori_loop(k * passes // (LINE - 1), (k + 1) * passes // (LINE - 1), student_pass, 0)
 
         return carry
 

time: 75.6 us -> 75.1 us (level)
  no operation moved by 1% of the time
where the time goes in v3:
time: 75.1 us; the launch traced here: 73.7 us
  Pallas kernels  69.4 us (92%)
  local copies, waits for them, and re-layouts  3.59 us (5%)
    pallas_call x1, Pallas kernels, fused(): pl.pallas_call(fused_kernel, out_shape=(jax.ShapeDtypeStruct((cols, token...  69.4 us
    unnamed x4, local copies, waits for them, and re-layouts  3.59 us

profile of v3, /device:TPU:0, one launch (start us, length us, event | category | flops | bytes accessed | tf_op | source)
XLA Modules:
  0.0 73.7 jit_solution(16192149760716277009)
XLA Ops:
  0.6 69.4 %shard_map.68 = (bf16[2000,512]{1,0:T(8,128)(2,1)}, f32[1,512]{1,0:T(1,128)}) custom-call(bf16[64,4608]{1,0:T(8,128)(2,1)} %hidden.1, s32[16]{0:T(128)} %route.1, bf16[2000,2304]{1,0:T(8,128)(2,1)} %bitcast.5, bf16[2000,512]{1,0:T(8,128)(2,1)} %bitcast.7, s32[1,512]{1,0:T(1,128)} %bitcast.8), custom_call_target="tpu_custom_call" | custom-call | tf_op jit(solution)/shard_map/pallas_call | solution.py:414
  70.1 0.0 copy-start
  70.1 3.0 %copy.9 = bf16[512,2000]{0,1:T(8,128)(2,1)} copy(bf16[512,2000]{0,1:T(8,128)(2,1)} %bitcast.6) | data formatting | bytes 4096000
  73.1 0.0 copy-done
  73.1 0.6 copy.10
Async XLA Ops:
  70.1 3.0 %copy-start = (f32[1,512]{1,0:T(1,128)S(1)}, f32[1,512]{1,0:T(1,128)}, u32[]{:S(2)}) copy-start(f32[1,512]{1,0:T(1,128)} %get-tuple-element.5) | copy-start | bytes 6148
